TPU v7x, 256 devices: a whole 4x4x8 slice. The times are simulated.
256 devices in a mesh: dp: 16 (over z_hi, y), seq: 16 (over x, z_lo, core).
Axes of the slice: x: 4, y: 4, z: 8 (z_hi: 4, z_lo: 2; z = z_hi * 2 + z_lo), core: 2. Of those that a mesh axis runs over, the one named last changes fastest.
Arguments:
- queries: bfloat16 [16, 2048, 2048], P('dp', 'seq'), may hold values from -12 to 12
- key_vectors: bfloat16 [16, 2304, 2048], P('dp', 'seq'), may hold values from -12 to 12
- value_vectors: bfloat16 [16, 2304, 2048], P('dp', 'seq'), may hold values from -24 to 24
- query_tangent: bfloat16 [16, 2048, 2048], P('dp', 'seq'), may hold values from -6 to 6
- key_tangent: bfloat16 [16, 2304, 2048], P('dp', 'seq'), may hold values from -6 to 6
- value_tangent: bfloat16 [16, 2304, 2048], P('dp', 'seq'), may hold values from -24 to 24
- latents: bfloat16 [16, 2048, 2048], P('dp', 'seq'), may hold values from -3 to 3
- latent_tangent: bfloat16 [16, 2048, 2048], P('dp', 'seq'), may hold values from -3 to 3
- modulation: bfloat16 [16, 2, 2048], P('dp'), may hold values from -2.5 to 2.5
- out_weight: bfloat16 [2048, 2048], P('dp'), may hold values from -0.125 to 0.125
Outputs:
- blended: bfloat16 [16, 2048, 2048], P('dp', 'seq')
- blended_tan: bfloat16 [16, 2048, 2048], P('dp', 'seq')
- weight_grad: float32 [2048, 2048], P('dp', 'seq')
All inputs are finite; a program needn't handle non-finite values.
Results may differ from a plain program's by a relative error of at most 0.011.
Values may be sent and summed in bfloat16 or wider, within the bound.
A program may use at most 128 MiB of HBM per device.

v0:
```python
import math

import jax
import jax.numpy as jnp
from jax import lax
from jax.sharding import PartitionSpec as P

HEAD = 64


def cross_scores(left, right):
    return lax.dot_general(
        left, right, (((1,), (1,)), ((), ())), preferred_element_type=jnp.float32
    )


def attend_block(query_rows, query_tan, key_rows, value_rows, key_tan, value_tan):
    factor = 1.0 / math.sqrt(HEAD)
    scores = cross_scores(query_rows, key_rows) * factor
    score_tan = (cross_scores(query_tan, key_rows) + cross_scores(query_rows, key_tan)) * factor
    row_peak = jnp.max(scores, axis=1, keepdims=True)
    shifted = jnp.exp(scores - row_peak)
    softmax = shifted / jnp.sum(shifted, axis=1, keepdims=True)
    softmax_low = softmax.astype(jnp.bfloat16)
    combined = jnp.dot(softmax_low, value_rows, preferred_element_type=jnp.float32)
    weighted = softmax * score_tan
    row_total = jnp.sum(weighted, axis=1, keepdims=True)
    weighted_low = weighted.astype(jnp.bfloat16)
    combined_tan = jnp.dot(weighted_low, value_rows, preferred_element_type=jnp.float32)
    combined_tan = combined_tan + jnp.dot(
        softmax_low, value_tan, preferred_element_type=jnp.float32
    )
    combined_tan = combined_tan - row_total * combined
    return (combined.astype(jnp.bfloat16), combined_tan.astype(jnp.bfloat16))


def block_length(count):
    for candidate in range(min(count, 1024), 0, -1):
        if count % candidate == 0:
            return candidate
    return count


def attend_heads(query_all, key_all, value_all, query_tan, key_tan, value_tan):
    total_rows = query_all.shape[0]
    heads_here = query_all.shape[1] // HEAD
    block = block_length(total_rows)
    outputs = []
    tangents = []
    for head in range(heads_here):
        lower = head * HEAD
        upper = lower + HEAD
        query_blocks = query_all[:, lower:upper].reshape(total_rows // block, block, HEAD)
        tan_blocks = query_tan[:, lower:upper].reshape(total_rows // block, block, HEAD)
        key_head = key_all[:, lower:upper]
        value_head = value_all[:, lower:upper]
        key_head_tan = key_tan[:, lower:upper]
        value_head_tan = value_tan[:, lower:upper]
        result = lax.map(
            lambda block_pair: attend_block(
                block_pair[0], block_pair[1], key_head, value_head, key_head_tan, value_head_tan
            ),
            (query_blocks, tan_blocks),
        )
        outputs.append(result[0].reshape(total_rows, HEAD))
        tangents.append(result[1].reshape(total_rows, HEAD))
    return (jnp.concatenate(outputs, axis=1), jnp.concatenate(tangents, axis=1))


def shards(
    queries,
    key_vectors,
    value_vectors,
    query_tangent,
    key_tangent,
    value_tangent,
    latents,
    latent_tangent,
    modulation,
    out_weight,
):
    arrived = (
        lax.all_to_all(queries, "seq", split_axis=2, concat_axis=1, tiled=True),
        lax.all_to_all(key_vectors, "seq", split_axis=2, concat_axis=1, tiled=True),
        lax.all_to_all(value_vectors, "seq", split_axis=2, concat_axis=1, tiled=True),
        lax.all_to_all(query_tangent, "seq", split_axis=2, concat_axis=1, tiled=True),
        lax.all_to_all(key_tangent, "seq", split_axis=2, concat_axis=1, tiled=True),
        lax.all_to_all(value_tangent, "seq", split_axis=2, concat_axis=1, tiled=True),
    )
    head_out, head_tan = attend_heads(
        arrived[0][0], arrived[1][0], arrived[2][0], arrived[3][0], arrived[4][0], arrived[5][0]
    )
    returned = lax.all_to_all(
        jnp.stack([head_out, head_tan]), "seq", split_axis=1, concat_axis=2, tiled=True
    )
    local_rows = returned.shape[1]
    stacked = returned.reshape(2 * local_rows, returned.shape[2])
    attn_out = stacked[:local_rows]
    projected = jnp.dot(
        stacked,
        lax.all_gather(out_weight, "dp", axis=0, tiled=True),
        preferred_element_type=jnp.float32,
    )
    proj = projected[:local_rows]
    proj_tan = projected[local_rows:]
    gate = modulation[0, 0].astype(jnp.float32)
    gate_tan = modulation[0, 1].astype(jnp.float32)
    blended = (latents[0].astype(jnp.float32) + gate * proj).astype(jnp.bfloat16)
    tangent_f = latent_tangent[0].astype(jnp.float32) + gate_tan * proj + gate * proj_tan
    length = jnp.sqrt(jnp.sum(tangent_f * tangent_f, axis=1, keepdims=True))
    direction = (gate * tangent_f / (length + 0.1)).astype(jnp.bfloat16)
    shares = lax.psum_scatter(
        -2.0
        * lax.dot_general(
            attn_out, direction, (((0,), (0,)), ((), ())), preferred_element_type=jnp.float32
        ),
        "dp",
        scatter_dimension=0,
        tiled=True,
    )
    weight_grad = lax.psum_scatter(shares, "seq", scatter_dimension=1, tiled=True)
    return (blended[None], tangent_f.astype(jnp.bfloat16)[None], weight_grad)


def solution(mesh):
    in_specs = (
        P("dp", "seq", None),
        P("dp", "seq", None),
        P("dp", "seq", None),
        P("dp", "seq", None),
        P("dp", "seq", None),
        P("dp", "seq", None),
        P("dp", "seq", None),
        P("dp", "seq", None),
        P("dp", None, None),
        P("dp", None),
    )
    out_specs = (P("dp", "seq", None), P("dp", "seq", None), P("dp", "seq"))
    return jax.shard_map(shards, mesh=mesh, in_specs=in_specs, out_specs=out_specs, check_vma=False)
```

profile of v0, /device:TPU:16, one launch (start us, length us, event | category | flops | bytes accessed | tf_op | source)
XLA Modules:
  0.0 608.3 jit_solution(9402165709158170943)
XLA Ops:
  7.2 2.4 copy.67
  10.1 11.4 %reduce = bf16[2048,128]{1,0:T(8,128)(2,1)S(1)} reduce(bf16[2048,1,128]{2,1,0:T(2,128)(2,1)S(1)} %bitcast.216, bf16[]{:T(256)} %broadcast.29), dimensions={1}, to_apply=%bitcast.105.reduce_sub_computation | reduce | bytes 1048578
  22.4 5.8 all-to-all-start
  28.2 2.4 copy.75
  30.5 11.4 %reduce.3 = bf16[2048,128]{1,0:T(8,128)(2,1)S(1)} reduce(bf16[2048,1,128]{2,1,0:T(2,128)(2,1)S(1)} %bitcast.217, bf16[]{:T(256)} %broadcast.29), dimensions={1}, to_apply=%bitcast.111.reduce_sub_computation | reduce | bytes 1048578
  43.7 6.0 all-to-all-start.3
  49.7 1.6 copy.69
  51.3 11.5 %reduce.2 = bf16[2048,144]{1,0:T(8,128)(2,1)S(1)} reduce(bf16[2048,1,144]{2,1,0:T(2,128)(2,1)S(1)} %bitcast.201, bf16[]{:T(256)} %broadcast.29), dimensions={1}, to_apply=%bitcast.107.reduce_sub_computation | reduce | bytes 1179650
  62.9 2.4 reshape.86
  65.3 5.9 all-to-all-start.1
  71.1 4.5 copy.72
  75.6 11.5 %reduce.1 = bf16[2048,144]{1,0:T(8,128)(2,1)S(1)} reduce(bf16[2048,1,144]{2,1,0:T(2,128)(2,1)S(1)} %bitcast.202, bf16[]{:T(256)} %broadcast.29), dimensions={1}, to_apply=%bitcast.109.reduce_sub_computation | reduce | bytes 1179650
  87.2 2.4 reshape.88
  89.6 6.1 %all-to-all-start.2 = ((bf16[16,2,9216]{2,1,0:T(2,128)(2,1)}), bf16[16,2,9216]{2,1,0:T(2,128)(2,1)}, u32[]{:S(2)}, u32[]{:S(2)}) async-start(bf16[16,2,9216]{2,1,0:T(2,128)(2,1)} %reshape.88), calls=%async_computation.2 | async-start | bytes 1179648 | tf_op jit(solution)/shard_map/all_to_all | solution.py:85
  95.7 4.5 copy.77
  100.2 11.5 %reduce.5 = bf16[2048,144]{1,0:T(8,128)(2,1)S(1)} reduce(bf16[2048,1,144]{2,1,0:T(2,128)(2,1)S(1)} %bitcast.203, bf16[]{:T(256)} %broadcast.29), dimensions={1}, to_apply=%bitcast.113.reduce_sub_computation | reduce | bytes 1179650
  111.8 2.4 reshape.92
  114.2 5.9 all-to-all-start.4
  120.8 4.5 copy.80
  125.3 11.5 %reduce.4 = bf16[2048,144]{1,0:T(8,128)(2,1)S(1)} reduce(bf16[2048,1,144]{2,1,0:T(2,128)(2,1)S(1)} %bitcast.196, bf16[]{:T(256)} %broadcast.29), dimensions={1}, to_apply=%bitcast.115.reduce_sub_computation | reduce | bytes 1179650
  136.8 2.4 reshape.94
  139.2 2.2 reshape.85
  141.8 2.2 reshape.91
  145.6 5.9 all-to-all-start.5
  152.6 5.5 reshape.87
  159.7 5.5 reshape.89
  165.2 3.3 copy.73
  170.8 5.5 reshape.93
  176.3 3.3 copy.78
  181.9 5.5 reshape.95
  187.3 3.3 copy.81
  192.1 2.9 fusion.81
  195.0 3.1 fusion.79
  198.8 43.0 %while.24 = (s32[]{:T(128)}, bf16[2,1024,64]{1,2,0:T(8,128)(2,1)S(1)}, bf16[2,1024,64]{1,2,0:T(8,128)(2,1)}, bf16[2,1024,64]{2,1,0:T(8,128)(2,1)}, bf16[2304,64]...) while((s32[]{:T(128)}, ...), condition=%wide.region_4.5_spmd, body=%wide.region_0.4_spmd.sunk | while | flops 1847653376 | bytes 104953088 | solution.py:59
  198.8 2.5 multiply_reduce_fusion.5
  201.4 1.7 fusion.140
  203.0 2.5 fusion.141
  206.9 5.5 fusion.143
  212.4 4.1 fusion.144
  220.4 2.4 multiply_reduce_fusion.5
  222.8 1.7 fusion.140
  224.5 2.5 fusion.141
  228.4 5.5 fusion.143
  233.8 4.1 fusion.144
  243.3 41.6 %while.25 = (s32[]{:T(128)}, bf16[2,1024,64]{1,2,0:T(8,128)(2,1)S(1)}, bf16[2,1024,64]{1,2,0:T(8,128)(2,1)}, bf16[2,1024,64]{2,1,0:T(8,128)(2,1)}, bf16[2304,64]...) while((s32[]{:T(128)}, ...), condition=%wide.region_9.10_spmd, body=%wide.region_5.9_spmd.sunk | while | flops 1847653376 | bytes 104658176 | solution.py:59
  243.5 2.4 multiply_reduce_fusion.6
  245.9 1.7 fusion.155
  247.6 2.5 fusion.156
  251.5 4.8 fusion.158
  256.4 4.0 fusion.159
  261.9 1.6 fusion.160
  264.2 2.4 multiply_reduce_fusion.6
  266.6 1.7 fusion.155
  268.3 2.5 fusion.156
  272.2 4.8 fusion.158
  277.1 4.0 fusion.159
  282.6 1.6 fusion.160
  288.0 2.0 copy.87
  290.0 6.0 all-to-all-start.6
  296.4 16.3 %all-to-all-done.6 = bf16[2,2048,128]{2,0,1:T(2,128)(2,1)S(1)} async-done(((bf16[2,2048,128]{2,0,1:T(2,128)(2,1)}), bf16[2,2048,128]{2,0,1:T(2,128)(2,1)S(1)}, u32[]{:S(2)}, u32[]{:S(2)}) %all-to-all-start.6) | async-done | bytes 1048608 | tf_op jit(solution)/shard_map/all_to_all | solution.py:93
  313.9 5.8 fusion.68
  320.9 8.2 %convolution_multiply_fusion = f32[2048,2048]{1,0:T(8,128)} fusion(bf16[128,2048]{0,1:T(8,128)(2,1)S(1)} %bitcast.218, f32[128,2048]{1,0:T(8,128)S(1)} %get-tuple-element.140, f32[128]{0:T(128)S(1)} %sqrt_add_fusion, f32[2048]{0:T(1024)S(1)} %bitcast.239), kind=kOutput, calls=%fused_computation.56 | convolution fusion | flops 1078722560 | bytes 18358784 | tf_op jit(solution)/shard_map/dot_general | solution.py:114
  329.1 206.4 %reduce-scatter.3.cloned.1.call-done = f32[128,2048]{1,0:T(8,128)} async-done(((f32[2048,2048]{1,0:T(8,128)}), f32[128,2048]{1,0:T(8,128)}) %reduce-scatter.3.cloned.1.call-update) | async-done | bytes 1048592 | tf_op jit(solution)/shard_map/reduce_scatter | solution.py:112
  536.4 64.9 %reduce-scatter.5.cloned.1.call-done = f32[128,128]{1,0:T(8,128)} async-done(((f32[128,2048]{1,0:T(8,128)}), f32[128,128]{1,0:T(8,128)}) %reduce-scatter.5.cloned.1.call-update) | async-done | bytes 65552 | tf_op jit(solution)/shard_map/reduce_scatter | solution.py:121
  (118 shorter events, 41.1 us)
Async XLA Ops:
  7.2 42.5 %copy-start.13 = (bf16[1,144,2048]{2,1,0:T(8,128)(2,1)S(1)}, bf16[1,144,2048]{2,1,0:T(8,128)(2,1)}, u32[]{:S(2)}) copy-start(bf16[1,144,2048]{2,1,0:T(8,128)(2,1)} %param.15) | copy-start | bytes 1769476
  22.4 20.5 %all-to-all-start = ((bf16[16,2,8192]{2,1,0:T(2,128)(2,1)}), bf16[16,2,8192]{2,1,0:T(2,128)(2,1)S(1)}, u32[]{:S(2)}, u32[]{:S(2)}) async-start(bf16[16,2,8192]{2,1,0:T(2,128)(2,1)} %reshape.84), calls=%async_computation | async-start | bytes 1048576 | tf_op jit(solution)/shard_map/all_to_all | solution.py:83
  42.9 0.8 copy-start.8
  43.7 21.6 %all-to-all-start.3 = ((bf16[16,2,8192]{2,1,0:T(2,128)(2,1)}), bf16[16,2,8192]{2,1,0:T(2,128)(2,1)}, u32[]{:S(2)}, u32[]{:S(2)}) async-start(bf16[16,2,8192]{2,1,0:T(2,128)(2,1)} %reshape.90), calls=%async_computation.3 | async-start | bytes 1048576 | tf_op jit(solution)/shard_map/all_to_all | solution.py:86
  65.3 24.3 %all-to-all-start.1 = ((bf16[16,2,9216]{2,1,0:T(2,128)(2,1)}), bf16[16,2,9216]{2,1,0:T(2,128)(2,1)}, u32[]{:S(2)}, u32[]{:S(2)}) async-start(bf16[16,2,9216]{2,1,0:T(2,128)(2,1)} %reshape.86), calls=%async_computation.1 | async-start | bytes 1179648 | tf_op jit(solution)/shard_map/all_to_all | solution.py:84
  89.6 24.6 %all-to-all-start.2 = ((bf16[16,2,9216]{2,1,0:T(2,128)(2,1)}), bf16[16,2,9216]{2,1,0:T(2,128)(2,1)}, u32[]{:S(2)}, u32[]{:S(2)}) async-start(bf16[16,2,9216]{2,1,0:T(2,128)(2,1)} %reshape.88), calls=%async_computation.2 | async-start | bytes 1179648 | tf_op jit(solution)/shard_map/all_to_all | solution.py:85
  114.2 31.4 %all-to-all-start.4 = ((bf16[16,2,9216]{2,1,0:T(2,128)(2,1)}), bf16[16,2,9216]{2,1,0:T(2,128)(2,1)}, u32[]{:S(2)}, u32[]{:S(2)}) async-start(bf16[16,2,9216]{2,1,0:T(2,128)(2,1)} %reshape.92), calls=%async_computation.4 | async-start | bytes 1179648 | tf_op jit(solution)/shard_map/all_to_all | solution.py:87
  120.1 193.8 %all-gather.2.cloned.1.call-start = ((), (), s32[]{:S(2)}) async-start(), calls=%async_computation.9 | async-start | bytes 8912896 | tf_op jit(solution)/shard_map/all_gather | solution.py:101
  145.6 36.3 %all-to-all-start.5 = ((bf16[16,2,9216]{2,1,0:T(2,128)(2,1)}), bf16[16,2,9216]{2,1,0:T(2,128)(2,1)}, u32[]{:S(2)}, u32[]{:S(2)}) async-start(bf16[16,2,9216]{2,1,0:T(2,128)(2,1)} %reshape.94), calls=%async_computation.5 | async-start | bytes 1179648 | tf_op jit(solution)/shard_map/all_to_all | solution.py:88
  198.8 44.5 %copy-start = (bf16[2304,64]{1,0:T(8,128)(2,1)S(1)}, bf16[2304,64]{1,0:T(8,128)(2,1)}, u32[]{:S(2)}) copy-start(bf16[2304,64]{1,0:T(8,128)(2,1)} %get-tuple-element.314) | copy-start | bytes 884740
  198.8 44.5 %copy-start.1 = (bf16[2304,64]{1,0:T(8,128)(2,1)S(1)}, bf16[2304,64]{1,0:T(8,128)(2,1)}, u32[]{:S(2)}) copy-start(bf16[2304,64]{1,0:T(8,128)(2,1)} %get-tuple-element.315) | copy-start | bytes 884740
  203.0 2.5 copy-start.7
  212.4 4.1 copy-start.2
  212.4 5.7 copy-start.5
  212.4 5.7 copy-start.11
  219.7 0.7 copy-start.12
  224.5 2.5 copy-start.7
  233.8 4.1 copy-start.2
  233.8 5.7 copy-start.5
  233.8 5.7 copy-start.11
  241.1 0.7 copy-start.12
  247.6 2.5 copy-start.6
  250.1 1.4 copy-start.4
  256.4 5.5 copy-start.3
  256.4 5.6 copy-start.9
  263.5 0.7 copy-start.10
  268.3 2.5 copy-start.6
  270.8 1.4 copy-start.4
  277.1 5.5 copy-start.3
  277.1 5.6 copy-start.9
  284.2 0.7 copy-start.10
  284.9 11.5 %copy-start.16 = (bf16[1,2,2048]{2,1,0:T(2,128)(2,1)S(1)}, bf16[1,2,2048]{2,1,0:T(2,128)(2,1)}, u32[]{:S(2)}) copy-start(bf16[1,2,2048]{2,1,0:T(2,128)(2,1)} %param.22) | copy-start | bytes 24580
  290.0 22.6 %all-to-all-start.6 = ((bf16[2,2048,128]{2,0,1:T(2,128)(2,1)}), bf16[2,2048,128]{2,0,1:T(2,128)(2,1)S(1)}, u32[]{:S(2)}, u32[]{:S(2)}) async-start(bf16[2,2048,128]{2,0,1:T(2,128)(2,1)} %copy.87), calls=%async_computation.6 | async-start | bytes 2097152 | tf_op jit(solution)/shard_map/all_to_all | solution.py:93
  296.1 239.4 %reduce-scatter.3.cloned.1.call-start = ((), (), s32[]{:S(2)}) async-start(), calls=%async_computation.10 | async-start | bytes 17825792 | tf_op jit(solution)/shard_map/reduce_scatter | solution.py:112
  313.8 5.8 copy-start.14
  313.9 5.8 copy-start.15
  329.1 272.2 %reduce-scatter.5.cloned.1.call-start = ((), (), s32[]{:S(2)}) async-start(), calls=%async_computation.11 | async-start | bytes 1114112 | tf_op jit(solution)/shard_map/reduce_scatter | solution.py:121
Sparse Core Ops, SparseCore 0:
  123.3 118.0 all-gather.1
  329.2 206.2 reduce-scatter.2
  538.6 62.6 reduce-scatter.4
where the time goes:
time: 619 us; the launch traced here: 608 us
  waiting for transfers between devices  288 us (47%)
  local copies, waits for them, and re-layouts  95.6 us (15%)
  other arithmetic  88.7 us (14%)
  matrix products  78.6 us (13%)
  starting transfers between devices  41.9 us (7%)
  between operations  14.6 us (2%)
    reduce_scatter x1, waiting for transfers between devices, shards(): lax.psum_scatter(-2.0 * lax.dot_general(attn_out, direction, (((0,), (0,)...  206 us
    unnamed x6, other arithmetic  69 us
    reduce_scatter x1, waiting for transfers between devices, shards(): lax.psum_scatter(shares, 'seq', scatter_dimension=1, tiled=True)  64.9 us
    unnamed x39, local copies, waits for them, and re-layouts  62.8 us
    dot_general x12, matrix products, cross_scores(): lax.dot_general(left, right, (((1,), (1,)), ((), ())), preferred_element_...  35.9 us
    all_to_all x1, waiting for transfers between devices, shards(): lax.all_to_all(jnp.stack([head_out, head_tan]), 'seq', split_axis=1, conc...  16.3 us
    dot_general x4, matrix products, attend_block(): jnp.dot(weighted_low, value_rows, preferred_element_type=jnp.float32)  16.2 us
  transfers between devices with their start and end apart: 10, of which 3 were waited for; matrix products, arithmetic and copies ran while one was open for 38% of the time, Pallas kernels for 0%

commit v1 on v0

v1 whole, which is shorter than its diff:
```python
import functools
import math

import jax
import jax.numpy as jnp
from jax import lax
from jax.experimental import pallas as pl
from jax.experimental.pallas import tpu as pltpu
from jax.sharding import PartitionSpec as P

MESH = pl.DeviceIdType.MESH
ANY = pl.BlockSpec(memory_space=pl.ANY)
VM = pl.BlockSpec(memory_space=pltpu.VMEM)
GROUP = 16
LANES = 128
HEAD = 64
TOK = 128
KEY_ROWS = 144
TOKENS = GROUP * TOK
KEYS = GROUP * KEY_ROWS
FEAT = 2048
BLOCK = 2 * TOK
TILE = 256
FACTOR = 1.0 / math.sqrt(HEAD)
EXP2_FACTOR = math.log2(math.e) * FACTOR


def dot(left, right):
    return jnp.dot(left, right, preferred_element_type=jnp.float32)


def dot_rows(left, right):
    return lax.dot_general(
        left, right, (((1,), (1,)), ((), ())), preferred_element_type=jnp.float32
    )


def dot_columns(left, right):
    return lax.dot_general(
        left, right, (((0,), (0,)), ((), ())), preferred_element_type=jnp.float32
    )


def lanes_of(index):
    return pl.ds(pl.multiple_of(index * LANES, LANES), LANES)


def rows_of(index, rows):
    return pl.ds(pl.multiple_of(index * rows, 16), rows)


def remote(src, dst, send, recv, device):
    return pltpu.make_async_remote_copy(
        src, dst, send, recv, device_id=device, device_id_type=MESH
    )


def attention_kernel(
    q, k, v, qt, kt, vt,
    ret, heads_out,
    q_in, k_in, v_in, qt_in, kt_in, vt_in,
    keys, values_a, values_b, lhs, scores, heads_tan,
    send, recv, recv_q, local, back_send, back_recv, back_local,
):
    me = lax.axis_index("seq")
    dp = lax.axis_index("dp")
    chip = me // 2
    sibling = jnp.bitwise_xor(me, 1)

    barrier = pltpu.get_barrier_semaphore()

    def greet(step, carry):
        pl.semaphore_signal(
            barrier, 1, device_id=(dp, jnp.bitwise_xor(me, step)), device_id_type=MESH
        )
        return carry

    lax.fori_loop(1, GROUP, greet, 0)
    pl.semaphore_wait(barrier, GROUP - 1)

    keyed = ((k, k_in), (kt, kt_in), (v, v_in), (vt, vt_in))
    queried = ((q, q_in), (qt, qt_in))

    def own(slot, src, dst, rows):
        return pltpu.make_async_copy(
            src.at[0, :, lanes_of(me)], dst.at[rows_of(me, rows), :], local.at[slot]
        )

    for slot, (src, dst) in enumerate(keyed):
        own(slot, src, dst, KEY_ROWS).start()

        def send_keys(step, carry, slot=slot, src=src, dst=dst):
            partner = jnp.bitwise_xor(me, step)
            remote(
                src.at[0, :, lanes_of(partner)], dst.at[rows_of(me, KEY_ROWS), :],
                send.at[slot], recv.at[slot], (dp, partner),
            ).start()
            return carry

        lax.fori_loop(1, GROUP, send_keys, 0)
    for slot, (src, dst) in enumerate(queried):
        own(4 + slot, src, dst, TOK).start()

    def send_queries(step, carry):
        partner = jnp.bitwise_xor(me, step)
        for slot, (src, dst) in enumerate(queried):
            remote(
                src.at[0, :, lanes_of(partner)], dst.at[rows_of(me, TOK), :],
                send.at[4 + slot], recv_q.at[chip], (dp, partner),
            ).start()
        return carry

    lax.fori_loop(1, GROUP, send_queries, 0)

    def all_keys(slot, dst):
        part = dst.at[pl.ds(0, (GROUP - 1) * KEY_ROWS), :]
        return remote(part, part, send.at[slot], recv.at[slot], (dp, sibling))

    lane = lax.broadcasted_iota(jnp.int32, (1, LANES), 1)
    low = lane < HEAD
    one = jnp.ones((), jnp.bfloat16)
    zero = jnp.zeros((), jnp.bfloat16)
    for slot, (src, dst) in enumerate(keyed):
        own(slot, src, dst, KEY_ROWS).wait()
        all_keys(slot, dst).wait_recv()
        if slot == 0:
            keys[:, :LANES] = k_in[...]
        elif slot == 1:
            keys[:, LANES:] = kt_in[...]
        elif slot == 2:
            values = v_in[...]
            values_a[:, :LANES] = jnp.where(low, values, one)
            values_b[:, :LANES] = jnp.where(low, one, values)
        else:
            values = vt_in[...]
            values_a[:, LANES:] = jnp.where(low, values, zero)
            values_b[:, LANES:] = jnp.where(low, zero, values)

    tiles = KEYS // TILE

    def block_scores(rows, head):
        mine = low if head == 0 else jnp.logical_not(low)
        query = jnp.where(mine, q_in[rows, :], zero)
        lhs[head, :BLOCK, :LANES] = query
        lhs[head, :BLOCK, LANES:] = jnp.zeros_like(query)
        lhs[head, BLOCK:, :LANES] = jnp.where(mine, qt_in[rows, :], zero)
        lhs[head, BLOCK:, LANES:] = query
        peak = None
        for tile in range(tiles):
            part = slice(tile * TILE, (tile + 1) * TILE)
            result = dot_rows(lhs[head], keys[part, :])
            scores[head, :, part] = result
            for column in range(TILE // LANES):
                piece = result[:BLOCK, column * LANES : (column + 1) * LANES]
                peak = piece if peak is None else jnp.maximum(peak, piece)
        return peak

    def block_values(head, peak):
        top = jnp.max(peak, axis=1, keepdims=True)
        values = (values_a, values_b)[head]
        total = None
        for tile in range(tiles):
            part = slice(tile * TILE, (tile + 1) * TILE)
            shifted = jnp.exp2((scores[head, :BLOCK, part] - top) * EXP2_FACTOR)
            weighted = shifted * scores[head, BLOCK:, part]
            pair = jnp.concatenate([shifted, weighted], 0).astype(jnp.bfloat16)
            term = dot(pair, values[part, :])
            total = term if total is None else total + term
        plain = total[:BLOCK, :LANES]
        tangent = total[BLOCK:, :LANES]
        inverse = 1.0 / pltpu.roll(plain, HEAD, 1)
        combined = plain * inverse
        row_total = pltpu.roll(tangent, HEAD, 1) * inverse
        combined_tan = (tangent * FACTOR + total[:BLOCK, LANES:]) * inverse
        return combined, combined_tan - FACTOR * row_total * combined

    def hand_back(partner):
        rows = rows_of(partner, TOK)
        pieces = ((heads_out, 0), (heads_tan, TOK))

        @pl.when(partner != me)
        def _():
            for held, place in pieces:
                remote(
                    held.at[rows, :], ret.at[pl.ds(place, TOK), lanes_of(me)],
                    back_send, back_recv, (dp, partner),
                ).start()

        @pl.when(partner == me)
        def _():
            for slot, (held, place) in enumerate(pieces):
                pltpu.make_async_copy(
                    held.at[rows, :], ret.at[pl.ds(place, TOK), lanes_of(me)],
                    back_local.at[slot],
                ).start()

    def body(step, carry):
        other = jnp.bitwise_xor(chip, step)

        @pl.when(step == 0)
        def _():
            for slot, (src, dst) in enumerate(queried):
                own(4 + slot, src, dst, TOK).wait()
            part = q_in.at[pl.ds(0, 2 * TOK), :]
            remote(part, part, send.at[4], recv_q.at[chip], (dp, sibling)).wait_recv()

        @pl.when(step > 0)
        def _():
            part = q_in.at[pl.ds(0, 4 * TOK), :]
            remote(part, part, send.at[4], recv_q.at[other], (dp, sibling)).wait_recv()

        rows = rows_of(other, BLOCK)
        peak_a = block_scores(rows, 0)
        peak_b = block_scores(rows, 1)
        out_a, tan_a = block_values(0, peak_a)
        out_b, tan_b = block_values(1, peak_b)
        heads_out[rows, :] = jnp.where(low, out_a, out_b).astype(jnp.bfloat16)
        heads_tan[rows, :] = jnp.where(low, tan_a, tan_b).astype(jnp.bfloat16)
        for core in range(2):
            hand_back(2 * other + core)
        return carry

    lax.fori_loop(0, GROUP // 2, body, 0)

    for slot, (src, dst) in enumerate(keyed):
        all_keys(slot, dst).wait_send()
    for slot, (src, dst) in enumerate(queried):
        part = dst.at[pl.ds(0, (GROUP - 1) * TOK), :]
        remote(part, part, send.at[4 + slot], recv_q.at[0], (dp, sibling)).wait_send()
    for slot, (held, place) in enumerate(((heads_out, 0), (heads_tan, TOK))):
        pltpu.make_async_copy(
            held.at[rows_of(me, TOK), :], ret.at[pl.ds(place, TOK), lanes_of(me)],
            back_local.at[slot],
        ).wait()
    part = ret.at[pl.ds(0, 2 * TOK * (GROUP - 1) // GROUP), :]
    back = remote(part, part, back_send, back_recv, (dp, sibling))
    back.wait_send()
    back.wait_recv()


def attention(q, k, v, qt, kt, vt):
    half = jnp.bfloat16
    return pl.pallas_call(
        attention_kernel,
        out_shape=[
            jax.ShapeDtypeStruct((2 * TOK, FEAT), half),
            jax.ShapeDtypeStruct((TOKENS, LANES), half),
        ],
        in_specs=[ANY] * 6,
        out_specs=[ANY, VM],
        scratch_shapes=[
            pltpu.VMEM((TOKENS, LANES), half),
            pltpu.VMEM((KEYS, LANES), half),
            pltpu.VMEM((KEYS, LANES), half),
            pltpu.VMEM((TOKENS, LANES), half),
            pltpu.VMEM((KEYS, LANES), half),
            pltpu.VMEM((KEYS, LANES), half),
            pltpu.VMEM((KEYS, 2 * LANES), half),
            pltpu.VMEM((KEYS, 2 * LANES), half),
            pltpu.VMEM((KEYS, 2 * LANES), half),
            pltpu.VMEM((2, 2 * BLOCK, 2 * LANES), half),
            pltpu.VMEM((2, 2 * BLOCK, KEYS), jnp.float32),
            pltpu.VMEM((TOKENS, LANES), half),
            pltpu.SemaphoreType.DMA((6,)),
            pltpu.SemaphoreType.DMA((4,)),
            pltpu.SemaphoreType.DMA((GROUP // 2,)),
            pltpu.SemaphoreType.DMA((6,)),
            pltpu.SemaphoreType.DMA,
            pltpu.SemaphoreType.DMA,
            pltpu.SemaphoreType.DMA((2,)),
        ],
        compiler_params=pltpu.CompilerParams(
            collective_id=0, has_side_effects=True, vmem_limit_bytes=56 * 2**20
        ),
        name="attention",
        cost_estimate=pl.CostEstimate(
            flops=7_250_000_000, bytes_accessed=10_000_000, transcendentals=9_437_184
        ),
    )(q, k, v, qt, kt, vt)


WCHUNK = 256
HALF_HEADS = 8


def output_kernel(
    ret, heads, weight, latents, latent_tan, modulation,
    blended_out, tan_out, grad_out,
    w_in, tangent, proj, direction, heads_in, dir_in, partial, shares,
    w_sem, a_local, a_send, a_recv, f_send, f_recv, d_send, d_recv, d_local,
    g_send, g_recv, g_local,
):
    me = lax.axis_index("seq")
    dp = lax.axis_index("dp")
    x = me // 4
    z = (me // 2) % 2
    core = me % 2
    sibling = jnp.bitwise_xor(me, 1)
    grad_z = (dp // 2) % 2
    grad_from = (me // 4) * 4 + grad_z * 2 + (me % 4) // 2
    grad_self = grad_from == me

    for chunk in range(FEAT // WCHUNK):
        part = pl.ds(chunk * WCHUNK, WCHUNK)
        pltpu.make_async_copy(weight.at[:, part], w_in.at[:, part], w_sem.at[chunk]).start()
    mine = 2 * x + core
    keep = pltpu.make_async_copy(heads, heads_in.at[:, lanes_of(mine)], a_local)
    keep.start()

    barrier = pltpu.get_barrier_semaphore()

    def greet(step, carry):
        pl.semaphore_signal(
            barrier, 1, device_id=(dp, jnp.bitwise_xor(me, step)), device_id_type=MESH
        )
        return carry

    lax.fori_loop(1, GROUP, greet, 0)

    def greet_grad(step, carry):
        @pl.when(jnp.logical_or(step != dp, jnp.logical_not(grad_self)))
        def _():
            pl.semaphore_signal(barrier, 1, device_id=(step, grad_from), device_id_type=MESH)

        return carry

    lax.fori_loop(0, GROUP, greet_grad, 0)
    pl.semaphore_wait(barrier, 2 * GROUP - 1 - grad_self.astype(jnp.int32))

    def spread(step):
        partner = jnp.bitwise_xor(me, 4 * step)
        return remote(
            heads, heads_in.at[:, lanes_of(mine)], a_send.at[step], a_recv.at[step], (dp, partner)
        )

    def forward(step):
        block = 2 * jnp.bitwise_xor(x, step) + core
        held = heads_in.at[:, lanes_of(block)]
        return remote(held, held, f_send.at[step], f_recv.at[step], (dp, sibling))

    for step in (1, 3, 2):
        spread(step).start()
    keep.wait()
    forward(0).start()

    gate = modulation[0, 0:1, :].astype(jnp.float32)
    gate_tan = modulation[0, 1:2, :].astype(jnp.float32)
    square = jnp.zeros((TOK, LANES), jnp.float32)
    for chunk in range(FEAT // WCHUNK):
        part = pl.ds(chunk * WCHUNK, WCHUNK)
        span = slice(chunk * WCHUNK, (chunk + 1) * WCHUNK)
        pltpu.make_async_copy(weight.at[:, part], w_in.at[:, part], w_sem.at[chunk]).wait()
        both = dot(ret[...], w_in[:, span])
        plain = both[:TOK]
        blended_out[0, :, span] = (
            latents[0, :, span].astype(jnp.float32) + gate[:, span] * plain
        ).astype(jnp.bfloat16)
        value = (
            latent_tan[0, :, span].astype(jnp.float32)
            + gate_tan[:, span] * plain
            + gate[:, span] * both[TOK:]
        )
        tangent[:, span] = value
        tan_out[0, :, span] = value.astype(jnp.bfloat16)
        power = value * value
        for column in range(WCHUNK // LANES):
            square = square + power[:, column * LANES : (column + 1) * LANES]
    length = jnp.sqrt(jnp.sum(square, axis=1, keepdims=True))
    scale = 1.0 / (length + 0.1)
    for chunk in range(FEAT // WCHUNK):
        span = slice(chunk * WCHUNK, (chunk + 1) * WCHUNK)
        direction[:, span] = (gate[:, span] * tangent[:, span] * scale).astype(jnp.bfloat16)

    def columns_for(partner):
        return pl.ds(pl.multiple_of((2 * (partner // 4) + partner % 2) * 256, 256), 256)

    def send_direction(step, carry):
        partner = jnp.bitwise_xor(me, step)
        remote(
            direction.at[:, columns_for(partner)], dir_in.at[rows_of(me, TOK), :],
            d_send, d_recv, (dp, partner),
        ).start()
        return carry

    lax.fori_loop(1, GROUP, send_direction, 0)
    own = pltpu.make_async_copy(
        direction.at[:, columns_for(me)], dir_in.at[rows_of(me, TOK), :], d_local
    )
    own.start()

    for step in (1, 3, 2):
        spread(step).wait_recv()
        forward(step).start()
    own.wait()
    part = dir_in.at[pl.ds(0, (GROUP - 1) * TOK), :]
    every = remote(part, part, d_send, d_recv, (dp, sibling))
    every.wait_recv()
    for step in range(4):
        forward(step).wait_recv()
    partial[...] = dot_columns(dir_in[...], heads_in[...]).astype(jnp.bfloat16)

    def share(block, column):
        row = 4 * (block // 2) + 2 * z + block % 2
        place = 4 * x + 2 * core + column
        return row, place, partial.at[pl.ds(column * LANES, LANES), lanes_of(block)]

    def send_shares(step, carry):
        block = jnp.bitwise_xor(step, 2 * x + core)
        for column in range(2):
            row, place, held = share(block, column)
            to_self = jnp.logical_and(row == dp, place == me)

            @pl.when(jnp.logical_not(to_self))
            def _():
                remote(held, shares.at[dp], g_send, g_recv, (row, place)).start()

            @pl.when(to_self)
            def _():
                pltpu.make_async_copy(held, shares.at[dp], g_local).start()

        return carry

    lax.fori_loop(0, HALF_HEADS, send_shares, 0)

    @pl.when(grad_self)
    def _():
        part = shares.at[pl.ds(0, GROUP - 1)]
        pltpu.make_async_copy(shares.at[0], shares.at[1], g_local).wait()
        whole = remote(part, part, g_send, g_recv, (dp, sibling))
        whole.wait_send()
        whole.wait_recv()

    @pl.when(jnp.logical_not(grad_self))
    def _():
        whole = remote(shares, shares, g_send, g_recv, (dp, sibling))
        whole.wait_send()
        whole.wait_recv()

    total = shares[0].astype(jnp.float32)
    for sample in range(1, GROUP):
        total = total + shares[sample].astype(jnp.float32)
    grad_out[...] = -2.0 * total.T

    every.wait_send()
    for step in (1, 3, 2):
        spread(step).wait_send()
    for step in range(4):
        forward(step).wait_send()


def output(ret, heads, weight, latents, latent_tan, modulation):
    half = jnp.bfloat16
    dma = pltpu.SemaphoreType.DMA
    return pl.pallas_call(
        output_kernel,
        out_shape=[
            jax.ShapeDtypeStruct((1, TOK, FEAT), half),
            jax.ShapeDtypeStruct((1, TOK, FEAT), half),
            jax.ShapeDtypeStruct((LANES, LANES), jnp.float32),
        ],
        in_specs=[VM, VM, ANY, VM, VM, VM],
        out_specs=[VM, VM, VM],
        scratch_shapes=[
            pltpu.VMEM((FEAT, FEAT), half),
            pltpu.VMEM((TOK, FEAT), jnp.float32),
            pltpu.VMEM((8, LANES), jnp.float32),
            pltpu.VMEM((TOK, FEAT), half),
            pltpu.VMEM((TOKENS, HALF_HEADS * LANES), half),
            pltpu.VMEM((TOKENS, 256), half),
            pltpu.VMEM((256, HALF_HEADS * LANES), half),
            pltpu.VMEM((GROUP, LANES, LANES), half),
            dma((FEAT // WCHUNK,)),
            dma, dma((4,)), dma((4,)), dma((4,)), dma((4,)), dma, dma, dma,
            dma, dma, dma,
        ],
        compiler_params=pltpu.CompilerParams(
            collective_id=1, has_side_effects=True, vmem_limit_bytes=56 * 2**20
        ),
        name="output",
        cost_estimate=pl.CostEstimate(
            flops=3_300_000_000, bytes_accessed=14_000_000, transcendentals=0
        ),
    )(ret, heads, weight, latents, latent_tan, modulation)


def shards(
    queries, key_vectors, value_vectors, query_tangent, key_tangent, value_tangent,
    latents, latent_tangent, modulation, out_weight,
):
    weight = lax.all_gather(out_weight, "dp", axis=0, tiled=True)
    ret, heads = attention(
        queries, key_vectors, value_vectors, query_tangent, key_tangent, value_tangent
    )
    return tuple(output(ret, heads, weight, latents, latent_tangent, modulation))


def solution(mesh):
    tokens = P("dp", "seq", None)
    in_specs = (tokens,) * 8 + (P("dp", None, None), P("dp", None))
    out_specs = (tokens, tokens, P("dp", "seq"))
    return jax.shard_map(
        shards, mesh=mesh, in_specs=in_specs, out_specs=out_specs, check_vma=False
    )
```

time: 619 us -> 224 us (0.36)
  the two profiles are of different devices: /device:TPU:16 before, /device:TPU:1 now
where the time goes in v1:
time: 224 us; the launch traced here: 221 us
  Pallas kernels  162 us (72%)
  waiting for transfers between devices  40 us (18%)
  between operations  14 us (6%)
  local copies, waits for them, and re-layouts  5.23 us (2%)
    pallas_call x1, Pallas kernels, attention(): pl.pallas_call(attention_kernel, out_shape=[jax.ShapeDtypeStruct((2 * TOK...  106 us
    pallas_call x1, Pallas kernels, output(): pl.pallas_call(output_kernel, out_shape=[jax.ShapeDtypeStruct((1, TOK, FE...  56 us
    all_gather x1, waiting for transfers between devices, shards(): weight = lax.all_gather(out_weight, 'dp', axis=0, tiled=True)  39.3 us
    unnamed x3, local copies, waits for them, and re-layouts  5.23 us
  transfers between devices with their start and end apart: 1, of which 1 were waited for; matrix products, arithmetic and copies ran while one was open for 0% of the time, Pallas kernels for 48%

profile of v1, /device:TPU:1, one launch (start us, length us, event | category | flops | bytes accessed | tf_op | source)
XLA Modules:
  0.0 221.0 jit_solution(5304227212535779374)
XLA Ops:
  7.2 0.0 all-gather.2.cloned.1.call-start
  7.2 0.7 all-gather.2.cloned.1.call-update
  7.9 105.7 %attention.1 = (bf16[256,2048]{1,0:T(8,128)(2,1)}, bf16[2048,128]{1,0:T(8,128)(2,1)}) custom-call(bf16[1,128,2048]{2,1,0:T(8,128)(2,1)} %q.1, bf16[1,144,2048]{2,1,0:T(8,128)(2,1)} %k.1, bf16[1,144,2048]{2,1,0:T(8,128)(2,1)} %v.1, bf16[1,128,2048]{2,1,0:T(8,128)(2,1)} %qt.1, bf16[1,144,2048]{2,1,0:T(8,128)(2,1)} %kt.1, bf16[1,144,2048]{2,1,0:T(8,128)(2,1)} %vt.1), custom_call_target="tpu_custom_call" | custom-call | flops 7249999872 | bytes 10000000 | tf_op jit(solution)/shard_map/attention/pallas_call | solution.py:243
  113.6 39.3 %all-gather.2.cloned.1.call-done.weight = bf16[2048,2048]{1,0:T(8,128)(2,1)} async-done(((bf16[128,2048]{1,0:T(8,128)(2,1)}), bf16[2048,2048]{1,0:T(8,128)(2,1)}) %all-gather.2.cloned.1.call-update) | async-done | bytes 8388624 | tf_op jit(solution)/shard_map/all_gather | solution.py:490
  152.9 56.0 %output.1 = (bf16[1,128,2048]{2,1,0:T(8,128)(2,1)}, bf16[1,128,2048]{2,1,0:T(8,128)(2,1)}, f32[128,128]{1,0:T(8,128)}) custom-call(bf16[256,2048]{1,0:T(8,128)(2,1)} %get-tuple-element.5.ret, bf16[2048,128]{1,0:T(8,128)(2,1)} %get-tuple-element.6.heads, bf16[2048,2048]{1,0:T(8,128)(2,1)} %all-gather.2.cloned.1.call-done.weight, ...), custom_call_target="tpu_custom_call" | custom-call | flops 3300000000 | bytes 14000000 | tf_op jit(solution)/shard_map/output/pallas_call | solution.py:454
  208.9 1.9 copy.16
  210.8 1.9 copy.17
  212.7 1.5 copy.18
Async XLA Ops:
  7.2 145.8 %all-gather.2.cloned.1.call-start = ((), (), s32[]{:S(2)}) async-start(), calls=%async_computation | async-start | bytes 8912896 | tf_op jit(solution)/shard_map/all_gather | solution.py:490
Sparse Core Ops, SparseCore 0:
  10.4 142.4 all-gather.1

commit v2 on v1

v2 whole, which is shorter than its diff:
```python
import functools
import math

import jax
import jax.numpy as jnp
from jax import lax
from jax.experimental import pallas as pl
from jax.experimental.pallas import tpu as pltpu
from jax.sharding import PartitionSpec as P

MESH = pl.DeviceIdType.MESH
ANY = pl.BlockSpec(memory_space=pl.ANY)
VM = pl.BlockSpec(memory_space=pltpu.VMEM)
GROUP = 16
LANES = 128
HEAD = 64
TOK = 128
KEY_ROWS = 144
TOKENS = GROUP * TOK
KEYS = GROUP * KEY_ROWS
FEAT = 2048
BLOCK = 2 * TOK
TILE = 256
FACTOR = 1.0 / math.sqrt(HEAD)
EXP2_FACTOR = math.log2(math.e) * FACTOR
WCHUNK = 256
BACK_ROWS = 2 * TOK * (GROUP - 1) // GROUP
COLUMNS = 512
EARLY = 6
QUARTER = FEAT // 4


def dot(left, right):
    return jnp.dot(left, right, preferred_element_type=jnp.float32)


def dot_rows(left, right):
    return lax.dot_general(
        left, right, (((1,), (1,)), ((), ())), preferred_element_type=jnp.float32
    )


def dot_columns(left, right):
    return lax.dot_general(
        left, right, (((0,), (0,)), ((), ())), preferred_element_type=jnp.float32
    )


def lanes_of(index):
    return pl.ds(pl.multiple_of(index * LANES, LANES), LANES)


def rows_of(index, rows):
    return pl.ds(pl.multiple_of(index * rows, 16), rows)


def heads_of(index):
    place = lax.rem(index, 4)
    return 4 * place + lax.rem(place + index // 4, 4)


def remote(src, dst, send, recv, device):
    return pltpu.make_async_remote_copy(
        src, dst, send, recv, device_id=device, device_id_type=MESH
    )


def whole_kernel(
    q, k, v, qt, kt, vt, latents_hbm, latent_tan_hbm, modulation, weight,
    blended_hbm, tan_hbm, grad_out,
    q_in, k_in, v_in, qt_in, kt_in, vt_in,
    keys, values_a, values_b, lhs, scores, heads_out, heads_tan, ret,
    w_in, latents, latent_tan, tangent, direction, heads_in, dir_in, partial, shares,
    send, recv, recv_q, local, back_send, back_recv, back_local,
    w_send, w_recv, w_forward, w_local, l_sem,
    a_local, a_send, a_recv, f_send, f_recv, d_send, d_recv, d_local,
    g_send, g_recv, g_local, crossed, c_send, c_recv,
    blended_out, tan_out, o_sem,
):
    me = lax.axis_index("seq")
    dp = lax.axis_index("dp")
    chip = me // 2
    x = me // 4
    z = (me // 2) % 2
    core = me % 2
    z_hi = dp // 4
    y = dp % 4
    sibling = jnp.bitwise_xor(me, 1)
    z_pair = jnp.bitwise_xor(me, 2)
    next_dp = 4 * lax.rem(z_hi + 2 * z + 3, 4) + y
    grad_from = 4 * lax.rem(y + 4 - z_hi, 4) + me % 4
    grad_self = grad_from == me

    barrier = pltpu.get_barrier_semaphore()

    def greet(step, carry):
        pl.semaphore_signal(
            barrier, 1, device_id=(dp, jnp.bitwise_xor(me, step)), device_id_type=MESH
        )
        return carry

    lax.fori_loop(1, GROUP, greet, 0)

    def greet_row(step, carry):
        pl.semaphore_signal(
            barrier, 1, device_id=(jnp.bitwise_xor(dp, step), me), device_id_type=MESH
        )
        return carry

    lax.fori_loop(1, 4, greet_row, 0)
    pl.semaphore_signal(barrier, 1, device_id=(next_dp, z_pair), device_id_type=MESH)

    keep_weight = pltpu.make_async_copy(weight, w_in.at[rows_of(dp, TOK), :], w_local)
    keep_weight.start()
    load_latents = pltpu.make_async_copy(latents_hbm, latents, l_sem.at[0])
    load_latents.start()
    load_tan = pltpu.make_async_copy(latent_tan_hbm, latent_tan, l_sem.at[1])
    load_tan.start()
    pl.semaphore_wait(barrier, GROUP - 1 + 4)

    half_rows = TOK // 2

    def weight_rows(block):
        return w_in.at[pl.ds(pl.multiple_of(block * TOK + core * half_rows, half_rows), half_rows), :]

    def send_weight(block, device):
        held = weight_rows(block)
        remote(held, held, w_send, w_recv.at[block], device).start()

    def wait_weight(block):
        held = weight_rows(block)
        remote(held, held, w_send, w_recv.at[block], (dp, sibling)).wait_recv()

    def send_weight_rows(block):
        def one(step, carry):
            send_weight(block, (jnp.bitwise_xor(dp, step), me))
            return carry

        lax.fori_loop(1, 4, one, 0)

    def forward_weight(block):
        held = weight_rows(block)
        remote(held, held, w_send, w_forward, (dp, sibling)).start()

    def forward_weight_rows(block):
        def one(step, carry):
            other = jnp.bitwise_xor(block, step)
            wait_weight(other)
            forward_weight(other)
            return carry

        lax.fori_loop(1, 4, one, 0)

    second = next_dp
    third = 4 * lax.rem(z_hi + 2 * (1 - z) + 3, 4) + y
    fourth = 4 * lax.rem(z_hi + 2, 4) + y

    keyed = ((k, k_in), (kt, kt_in), (v, v_in), (vt, vt_in))
    queried = ((q, q_in), (qt, qt_in))

    def own(slot, src, dst, rows):
        return pltpu.make_async_copy(
            src.at[0, :, lanes_of(heads_of(me))], dst.at[rows_of(me, rows), :], local.at[slot]
        )

    keep_weight.wait()
    send_weight(dp, (next_dp, z_pair))
    for slot, (src, dst) in enumerate(keyed):
        own(slot, src, dst, KEY_ROWS).start()

        def send_keys(step, carry, slot=slot, src=src, dst=dst):
            partner = jnp.bitwise_xor(me, step)
            remote(
                src.at[0, :, lanes_of(heads_of(partner))], dst.at[rows_of(me, KEY_ROWS), :],
                send.at[slot], recv.at[slot], (dp, partner),
            ).start()
            return carry

        lax.fori_loop(1, GROUP, send_keys, 0)
        if slot == 1:
            send_weight_rows(dp)
            wait_weight(second)
            send_weight(second, (dp, z_pair))
            send_weight_rows(second)
    for slot, (src, dst) in enumerate(queried):
        own(4 + slot, src, dst, TOK).start()

    def send_queries(step, carry):
        partner = jnp.bitwise_xor(me, step)
        for slot, (src, dst) in enumerate(queried):
            remote(
                src.at[0, :, lanes_of(heads_of(partner))], dst.at[rows_of(me, TOK), :],
                send.at[4 + slot], recv_q.at[chip], (dp, partner),
            ).start()
        return carry

    lax.fori_loop(1, GROUP, send_queries, 0)

    def all_keys(slot, dst):
        part = dst.at[pl.ds(0, (GROUP - 1) * KEY_ROWS), :]
        return remote(part, part, send.at[slot], recv.at[slot], (dp, sibling))

    lane = lax.broadcasted_iota(jnp.int32, (1, LANES), 1)
    low = lane < HEAD
    one = jnp.ones((), jnp.bfloat16)
    zero = jnp.zeros((), jnp.bfloat16)
    for slot, (src, dst) in enumerate(keyed):
        own(slot, src, dst, KEY_ROWS).wait()
        all_keys(slot, dst).wait_recv()
        if slot == 0:
            keys[:, :LANES] = k_in[...]
            forward_weight(second)
            wait_weight(third)
            send_weight(third, (next_dp, z_pair))
            send_weight_rows(third)
            forward_weight(third)
        elif slot == 1:
            keys[:, LANES:] = kt_in[...]
        elif slot == 2:
            values = v_in[...]
            values_a[:, :LANES] = jnp.where(low, values, one)
            values_b[:, :LANES] = jnp.where(low, one, values)
            wait_weight(fourth)
            send_weight_rows(fourth)
            forward_weight(fourth)
        else:
            values = vt_in[...]
            values_a[:, LANES:] = jnp.where(low, values, zero)
            values_b[:, LANES:] = jnp.where(low, zero, values)

    tiles = KEYS // TILE

    def block_scores(rows, head):
        mine = low if head == 0 else jnp.logical_not(low)
        query = jnp.where(mine, q_in[rows, :], zero)
        lhs[head, :BLOCK, :LANES] = query
        lhs[head, :BLOCK, LANES:] = jnp.zeros_like(query)
        lhs[head, BLOCK:, :LANES] = jnp.where(mine, qt_in[rows, :], zero)
        lhs[head, BLOCK:, LANES:] = query
        peak = None
        for tile in range(tiles):
            part = slice(tile * TILE, (tile + 1) * TILE)
            result = dot_rows(lhs[head], keys[part, :])
            scores[head, :, part] = result
            for column in range(TILE // LANES):
                piece = result[:BLOCK, column * LANES : (column + 1) * LANES]
                peak = piece if peak is None else jnp.maximum(peak, piece)
        return peak

    def block_values(head, peak):
        top = jnp.max(peak, axis=1, keepdims=True)
        values = (values_a, values_b)[head]
        total = None
        for tile in range(tiles):
            part = slice(tile * TILE, (tile + 1) * TILE)
            shifted = jnp.exp2((scores[head, :BLOCK, part] - top) * EXP2_FACTOR)
            weighted = shifted * scores[head, BLOCK:, part]
            pair = jnp.concatenate([shifted, weighted], 0).astype(jnp.bfloat16)
            term = dot(pair, values[part, :])
            total = term if total is None else total + term
        plain = total[:BLOCK, :LANES]
        tangent = total[BLOCK:, :LANES]
        inverse = 1.0 / pltpu.roll(plain, HEAD, 1)
        combined = plain * inverse
        row_total = pltpu.roll(tangent, HEAD, 1) * inverse
        combined_tan = (tangent * FACTOR + total[:BLOCK, LANES:]) * inverse
        return combined, combined_tan - FACTOR * row_total * combined

    place = me % 4

    def hand_over(rows):
        remote(
            heads_out.at[rows, :], heads_in.at[rows, lanes_of(place)], a_send, a_recv, (dp, z_pair)
        ).start()

    def hand_back(partner):
        rows = rows_of(partner, TOK)
        pieces = ((heads_out, 0), (heads_tan, TOK))

        @pl.when(partner != me)
        def _():
            for held, first in pieces:
                remote(
                    held.at[rows, :], ret.at[pl.ds(first, TOK), lanes_of(heads_of(me))],
                    back_send, back_recv, (dp, partner),
                ).start()

        @pl.when(partner == me)
        def _():
            for slot, (held, first) in enumerate(pieces):
                pltpu.make_async_copy(
                    held.at[rows, :], ret.at[pl.ds(first, TOK), lanes_of(heads_of(me))],
                    back_local.at[slot],
                ).start()

    def body(step, carry):
        other = jnp.bitwise_xor(chip, step)

        @pl.when(step == 0)
        def _():
            for slot, (src, dst) in enumerate(queried):
                own(4 + slot, src, dst, TOK).wait()
            part = q_in.at[pl.ds(0, 2 * TOK), :]
            remote(part, part, send.at[4], recv_q.at[chip], (dp, sibling)).wait_recv()

        @pl.when(step > 0)
        def _():
            part = q_in.at[pl.ds(0, 4 * TOK), :]
            remote(part, part, send.at[4], recv_q.at[other], (dp, sibling)).wait_recv()

        @pl.when(step == 2)
        def _():
            forward_weight_rows(dp)

        @pl.when(step == 4)
        def _():
            forward_weight_rows(second)

        @pl.when(step == 6)
        def _():
            forward_weight_rows(third)

        rows = rows_of(other, BLOCK)
        peak_a = block_scores(rows, 0)
        peak_b = block_scores(rows, 1)
        out_a, tan_a = block_values(0, peak_a)
        out_b, tan_b = block_values(1, peak_b)
        heads_out[rows, :] = jnp.where(low, out_a, out_b).astype(jnp.bfloat16)
        heads_tan[rows, :] = jnp.where(low, tan_a, tan_b).astype(jnp.bfloat16)
        for side in range(2):
            hand_back(2 * other + side)
        heads_in[rows, lanes_of(place)] = heads_out[rows, :]

        @pl.when(step < EARLY)
        def _():
            hand_over(rows)

        return carry

    lax.fori_loop(0, GROUP // 2, body, 0)

    for slot, (held, first) in enumerate(((heads_out, 0), (heads_tan, TOK))):
        pltpu.make_async_copy(
            held.at[rows_of(me, TOK), :], ret.at[pl.ds(first, TOK), lanes_of(heads_of(me))],
            back_local.at[slot],
        ).wait()


    def hand_rest(step, carry):
        hand_over(rows_of(jnp.bitwise_xor(chip, step), BLOCK))
        return carry

    lax.fori_loop(EARLY, GROUP // 2, hand_rest, 0)
    cross_heads = remote(heads_out, heads_in.at[:, lanes_of(place)], a_send, a_recv, (dp, z_pair))

    def forward(slot, block):
        held = heads_in.at[:, lanes_of(block)]
        return remote(held, held, f_send.at[slot], f_recv.at[slot], (dp, sibling))

    forward(0, place).start()
    forward_weight_rows(fourth)
    part = w_in.at[pl.ds(0, (GROUP - 1) * half_rows), :]
    remote(part, part, w_send, w_forward, (dp, sibling)).wait_recv()
    load_latents.wait()
    load_tan.wait()
    back = remote(
        ret.at[pl.ds(0, BACK_ROWS), :], ret.at[pl.ds(0, BACK_ROWS), :],
        back_send, back_recv, (dp, sibling),
    )
    back.wait_recv()

    gate = modulation[0, 0:1, :].astype(jnp.float32)
    gate_tan = modulation[0, 1:2, :].astype(jnp.float32)
    square = jnp.zeros((TOK, LANES), jnp.float32)
    for chunk in range(FEAT // WCHUNK):
        span = slice(chunk * WCHUNK, (chunk + 1) * WCHUNK)
        both = dot(ret[...], w_in[:, span])
        plain = both[:TOK]
        blended_out[0, :, span] = (
            latents[0, :, span].astype(jnp.float32) + gate[:, span] * plain
        ).astype(jnp.bfloat16)
        value = (
            latent_tan[0, :, span].astype(jnp.float32)
            + gate_tan[:, span] * plain
            + gate[:, span] * both[TOK:]
        )
        tangent[:, span] = value
        tan_out[0, :, span] = value.astype(jnp.bfloat16)
        power = value * value
        for column in range(WCHUNK // LANES):
            square = square + power[:, column * LANES : (column + 1) * LANES]
    store_blended = pltpu.make_async_copy(blended_out, blended_hbm, o_sem.at[0])
    store_blended.start()
    store_tan = pltpu.make_async_copy(tan_out, tan_hbm, o_sem.at[1])
    store_tan.start()
    length = jnp.sqrt(jnp.sum(square, axis=1, keepdims=True))
    scale = 1.0 / (length + 0.1)
    for chunk in range(FEAT // WCHUNK):
        span = slice(chunk * WCHUNK, (chunk + 1) * WCHUNK)
        rounded = (gate[:, span] * tangent[:, span] * scale).astype(jnp.bfloat16)
        for column in range(WCHUNK // LANES):
            block = chunk * (WCHUNK // LANES) + column
            spot = (block % 4) * COLUMNS + (block // 4) * LANES
            direction[:, spot : spot + LANES] = rounded[:, column * LANES : (column + 1) * LANES]

    def piece(group, part):
        return pl.ds(pl.multiple_of(group * COLUMNS, COLUMNS) + part * LANES, LANES)

    def cross(part, side):
        return remote(
            direction.at[:, piece(2 * (1 - z) + side, part)], crossed.at[:, piece(side, part)],
            c_send, c_recv.at[part], (dp, z_pair),
        )

    def cross_wait(part):
        both = crossed.at[:, pl.ds(0, 2 * LANES)]
        return remote(both, both, c_send, c_recv.at[part], (dp, z_pair))

    def spread(part, mine):
        source = me if mine else z_pair

        def one(step, carry):
            partner = jnp.bitwise_xor(me, 4 * (step // 2) + step % 2)
            if mine:
                held = direction.at[:, piece(2 * z + partner % 2, part)]
            else:
                held = crossed.at[:, piece(partner % 2, part)]
            remote(
                held, dir_in.at[rows_of(source, TOK), pl.ds(part * LANES, LANES)],
                d_send, d_recv.at[part], (dp, partner),
            ).start()
            return carry

        lax.fori_loop(1, 8, one, 0)

    def keep_part(part, mine):
        source = me if mine else z_pair
        held = direction.at[:, piece(me % 4, part)] if mine else crossed.at[:, piece(core, part)]
        return pltpu.make_async_copy(
            held, dir_in.at[rows_of(source, TOK), pl.ds(part * LANES, LANES)],
            d_local.at[part, int(mine)],
        )

    def pass_on(part):
        cross_wait(part).wait_recv()
        spread(part, False)
        keep_part(part, False).start()

    for part in range(4):
        for side in range(2):
            cross(part, side).start()
    for part in range(4):
        spread(part, True)
        keep_part(part, True).start()
        if part >= 1:
            pass_on(part - 1)
    pass_on(3)

    cross_heads.wait_recv()
    forward(1, jnp.bitwise_xor(place, 2)).start()
    forward(0, place).wait_recv()
    forward(1, place).wait_recv()

    for part in range(4):
        span = slice(part * LANES, (part + 1) * LANES)
        keep_part(part, True).wait()
        keep_part(part, False).wait()
        every = dir_in.at[pl.ds(0, (GROUP - 2) * TOK), pl.ds(0, LANES)]
        remote(every, every, d_send, d_recv.at[part], (dp, sibling)).wait_recv()
        partial[span, :] = dot_columns(dir_in[:, span], heads_in[...]).astype(jnp.bfloat16)
        owner = 4 * part + me % 4

        def send_shares(step, carry, part=part, owner=owner):
            block = jnp.bitwise_xor(step, z_hi)
            row = heads_of(4 * x + block)
            held = partial.at[pl.ds(part * LANES, LANES), lanes_of(block)]
            to_self = jnp.logical_and(row == dp, owner == me)

            @pl.when(jnp.logical_not(to_self))
            def _():
                remote(held, shares.at[dp], g_send, g_recv, (row, owner)).start()

            @pl.when(to_self)
            def _():
                pltpu.make_async_copy(held, shares.at[dp], g_local).start()

            return carry

        lax.fori_loop(0, 4, send_shares, 0)

    @pl.when(grad_self)
    def _():
        part = shares.at[pl.ds(0, GROUP - 1)]
        pltpu.make_async_copy(shares.at[0], shares.at[1], g_local).wait()
        whole = remote(part, part, g_send, g_recv, (dp, sibling))
        whole.wait_send()
        whole.wait_recv()

    @pl.when(jnp.logical_not(grad_self))
    def _():
        whole = remote(shares, shares, g_send, g_recv, (dp, sibling))
        whole.wait_send()
        whole.wait_recv()

    store_blended.wait()
    store_tan.wait()
    total = shares[0].astype(jnp.float32)
    for sample in range(1, GROUP):
        total = total + shares[sample].astype(jnp.float32)
    grad_out[...] = -2.0 * total.T

    every = dir_in.at[pl.ds(0, (GROUP - 2) * TOK), :]
    remote(every, every, d_send, d_recv.at[0], (dp, sibling)).wait_send()
    remote(crossed, crossed, c_send, c_recv.at[0], (dp, z_pair)).wait_send()
    cross_heads.wait_send()
    forward(0, place).wait_send()
    forward(1, place).wait_send()
    back.wait_send()
    part = w_in.at[pl.ds(0, 2 * (GROUP - 1) * half_rows), :]
    remote(part, part, w_send, w_forward, (dp, sibling)).wait_send()
    for slot, (src, dst) in enumerate(keyed):
        all_keys(slot, dst).wait_send()
    for slot, (src, dst) in enumerate(queried):
        part = dst.at[pl.ds(0, (GROUP - 1) * TOK), :]
        remote(part, part, send.at[4 + slot], recv_q.at[0], (dp, sibling)).wait_send()


def whole(*args):
    half = jnp.bfloat16
    dma = pltpu.SemaphoreType.DMA
    vmem = pltpu.VMEM
    return pl.pallas_call(
        whole_kernel,
        out_shape=[
            jax.ShapeDtypeStruct((1, TOK, FEAT), half),
            jax.ShapeDtypeStruct((1, TOK, FEAT), half),
            jax.ShapeDtypeStruct((LANES, LANES), jnp.float32),
        ],
        in_specs=[ANY] * 8 + [VM, ANY],
        out_specs=[ANY, ANY, VM],
        scratch_shapes=[
            vmem((TOKENS, LANES), half),
            vmem((KEYS, LANES), half),
            vmem((KEYS, LANES), half),
            vmem((TOKENS, LANES), half),
            vmem((KEYS, LANES), half),
            vmem((KEYS, LANES), half),
            vmem((KEYS, 2 * LANES), half),
            vmem((KEYS, 2 * LANES), half),
            vmem((KEYS, 2 * LANES), half),
            vmem((2, 2 * BLOCK, 2 * LANES), half),
            vmem((2, 2 * BLOCK, KEYS), jnp.float32),
            vmem((TOKENS, LANES), half),
            vmem((TOKENS, LANES), half),
            vmem((2 * TOK, FEAT), half),
            vmem((FEAT, FEAT), half),
            vmem((1, TOK, FEAT), half),
            vmem((1, TOK, FEAT), half),
            vmem((TOK, FEAT), jnp.float32),
            vmem((TOK, FEAT), half),
            vmem((TOKENS, QUARTER), half),
            vmem((TOKENS, COLUMNS), half),
            vmem((COLUMNS, QUARTER), half),
            vmem((GROUP, LANES, LANES), half),
            dma((6,)), dma((4,)), dma((GROUP // 2,)), dma((6,)), dma, dma, dma((2,)),
            dma, dma((GROUP,)), dma, dma, dma((2,)),
            dma, dma, dma, dma((2,)), dma((2,)), dma, dma((4,)), dma((4, 2)),
            dma, dma, dma, vmem((TOK, 2 * COLUMNS), half), dma, dma((4,)),
            vmem((1, TOK, FEAT), half), vmem((1, TOK, FEAT), half), dma((2,)),
        ],
        compiler_params=pltpu.CompilerParams(
            collective_id=0, has_side_effects=True, vmem_limit_bytes=56 * 2**20
        ),
        name="whole",
        cost_estimate=pl.CostEstimate(
            flops=10_500_000_000, bytes_accessed=20_000_000, transcendentals=9_437_184
        ),
    )(*args)


def finish_kernel(*refs):
    count = len(refs) // 2
    for index in range(count):
        refs[count + index][...] = refs[index][...]


def finish(arrays):
    return tuple(
        pl.pallas_call(
            finish_kernel,
            out_shape=[jax.ShapeDtypeStruct(array.shape, array.dtype) for array in arrays],
            in_specs=[VM] * len(arrays),
            out_specs=[VM] * len(arrays),
            name="finish",
        )(*arrays)
    )


def shards(
    queries, key_vectors, value_vectors, query_tangent, key_tangent, value_tangent,
    latents, latent_tangent, modulation, out_weight,
):
    return finish(
        whole(
            queries, key_vectors, value_vectors, query_tangent, key_tangent, value_tangent,
            latents, latent_tangent, modulation, out_weight,
        )
    )


def solution(mesh):
    tokens = P("dp", "seq", None)
    in_specs = (tokens,) * 8 + (P("dp", None, None), P("dp", None))
    out_specs = (tokens, tokens, P("dp", "seq"))
    return jax.shard_map(
        shards, mesh=mesh, in_specs=in_specs, out_specs=out_specs, check_vma=False
    )
```

time: 224 us -> 123 us (0.55)
  the two profiles are of different devices: /device:TPU:1 before, /device:TPU:6 now
where the time goes in v2:
time: 123 us
  Pallas kernels  122 us (99%)
    pallas_call x1, Pallas kernels, whole(): pl.pallas_call(whole_kernel, out_shape=[jax.ShapeDtypeStruct((1, TOK, FEA...  120 us

profile of v2, /device:TPU:6, one launch (start us, length us, event | category | flops | bytes accessed | tf_op | source)
XLA Modules:
  0.0 122.7 jit_solution(17889642348940281767)
XLA Ops:
  0.6 119.9 %whole.1 = (bf16[1,128,2048]{2,1,0:T(8,128)(2,1)}, bf16[1,128,2048]{2,1,0:T(8,128)(2,1)}, f32[128,128]{1,0:T(8,128)}) custom-call(bf16[1,128,2048]{2,1,0:T(8,128)(2,1)} %q.1, bf16[1,144,2048]{2,1,0:T(8,128)(2,1)} %k.1, bf16[1,144,2048]{2,1,0:T(8,128)(2,1)} %v.1, bf16[1,128,2048]{2,1,0:T(8,128)(2,1)} %qt.1, bf16[1,144,2048]{2,1,0:T(8,128)(2,1)} %kt.1, ...), custom_call_target="tpu_custom_call" | custom-call | flops 10499999744 | bytes 20000000 | tf_op jit(solution)/shard_map/whole/pallas_call | solution.py:532
  120.5 2.2 %finish.1 = (bf16[1,128,2048]{2,1,0:T(8,128)(2,1)}, bf16[1,128,2048]{2,1,0:T(8,128)(2,1)}, f32[128,128]{1,0:T(8,128)}) custom-call(bf16[1,128,2048]{2,1,0:T(8,128)(2,1)} %get-tuple-element.6.refs_0_, bf16[1,128,2048]{2,1,0:T(8,128)(2,1)} %get-tuple-element.7.refs_1_, f32[128,128]{1,0:T(8,128)} %get-tuple-element.8.refs_2_), custom_call_target="tpu_custom_call" | custom-call | tf_op jit(solution)/shard_map/finish/pallas_call | solution.py:589

commit v3 on v2

--- a/solution.py
+++ b/solution.py
@@ -25,9 +25,10 @@
 EXP2_FACTOR = math.log2(math.e) * FACTOR
 WCHUNK = 256
 BACK_ROWS = 2 * TOK * (GROUP - 1) // GROUP
-COLUMNS = 512
+HALF_HEADS = 8
+SUMS = 4
+PARTS = 2
 EARLY = 6
-QUARTER = FEAT // 4
 
 
 def dot(left, right):
@@ -55,8 +56,8 @@
 
 
 def heads_of(index):
-    place = lax.rem(index, 4)
-    return 4 * place + lax.rem(place + index // 4, 4)
+    row = index // 4
+    return 4 * row + lax.rem(2 * (index % 2) + (index // 2) % 2 + row, 4)
 
 
 def remote(src, dst, send, recv, device):
@@ -74,8 +75,8 @@
     send, recv, recv_q, local, back_send, back_recv, back_local,
     w_send, w_recv, w_forward, w_local, l_sem,
     a_local, a_send, a_recv, f_send, f_recv, d_send, d_recv, d_local,
-    g_send, g_recv, g_local, crossed, c_send, c_recv,
-    blended_out, tan_out, o_sem,
+    g_send, g_recv, g_local,
+    blended_out, tan_out, o_sem, stage_in, middle, h_send, h_recv,
 ):
     me = lax.axis_index("seq")
     dp = lax.axis_index("dp")
@@ -88,7 +89,7 @@
     sibling = jnp.bitwise_xor(me, 1)
     z_pair = jnp.bitwise_xor(me, 2)
     next_dp = 4 * lax.rem(z_hi + 2 * z + 3, 4) + y
-    grad_from = 4 * lax.rem(y + 4 - z_hi, 4) + me % 4
+    grad_from = 4 * x + 2 * ((y + z_hi) % 2) + z
     grad_self = grad_from == me
 
     barrier = pltpu.get_barrier_semaphore()
@@ -165,8 +166,14 @@
 
     keep_weight.wait()
     send_weight(dp, (next_dp, z_pair))
+    def all_keys(slot, dst):
+        part = dst.at[pl.ds(0, (GROUP - 1) * KEY_ROWS), :]
+        return remote(part, part, send.at[slot], recv.at[slot], (dp, sibling))
+
     for slot, (src, dst) in enumerate(keyed):
         own(slot, src, dst, KEY_ROWS).start()
+        if slot >= 2:
+            all_keys(slot - 2, keyed[slot - 2][1]).wait_send()
 
         def send_keys(step, carry, slot=slot, src=src, dst=dst):
             partner = jnp.bitwise_xor(me, step)
@@ -185,6 +192,8 @@
     for slot, (src, dst) in enumerate(queried):
         own(4 + slot, src, dst, TOK).start()
 
+    all_keys(2, v_in).wait_send()
+
     def send_queries(step, carry):
         partner = jnp.bitwise_xor(me, step)
         for slot, (src, dst) in enumerate(queried):
@@ -195,10 +204,6 @@
         return carry
 
     lax.fori_loop(1, GROUP, send_queries, 0)
-
-    def all_keys(slot, dst):
-        part = dst.at[pl.ds(0, (GROUP - 1) * KEY_ROWS), :]
-        return remote(part, part, send.at[slot], recv.at[slot], (dp, sibling))
 
     lane = lax.broadcasted_iota(jnp.int32, (1, LANES), 1)
     low = lane < HEAD
@@ -266,12 +271,14 @@
         combined_tan = (tangent * FACTOR + total[:BLOCK, LANES:]) * inverse
         return combined, combined_tan - FACTOR * row_total * combined
 
-    place = me % 4
+    place = 2 * x + core
 
     def hand_over(rows):
-        remote(
-            heads_out.at[rows, :], heads_in.at[rows, lanes_of(place)], a_send, a_recv, (dp, z_pair)
-        ).start()
+        for step in (2, 1, 3):
+            remote(
+                heads_out.at[rows, :], heads_in.at[rows, lanes_of(place)],
+                a_send.at[step], a_recv.at[step], (dp, jnp.bitwise_xor(me, 4 * step)),
+            ).start()
 
     def hand_back(partner):
         rows = rows_of(partner, TOK)
@@ -351,13 +358,17 @@
         return carry
 
     lax.fori_loop(EARLY, GROUP // 2, hand_rest, 0)
-    cross_heads = remote(heads_out, heads_in.at[:, lanes_of(place)], a_send, a_recv, (dp, z_pair))
-
-    def forward(slot, block):
-        held = heads_in.at[:, lanes_of(block)]
-        return remote(held, held, f_send.at[slot], f_recv.at[slot], (dp, sibling))
-
-    forward(0, place).start()
+    def handed(step):
+        return remote(
+            heads_out, heads_in.at[:, lanes_of(place)], a_send.at[step], a_recv.at[step],
+            (dp, jnp.bitwise_xor(me, 4 * step)),
+        )
+
+    def forward(step):
+        held = heads_in.at[:, lanes_of(2 * jnp.bitwise_xor(x, step) + core)]
+        return remote(held, held, f_send.at[step], f_recv.at[step], (dp, sibling))
+
+    forward(0).start()
     forward_weight_rows(fourth)
     part = w_in.at[pl.ds(0, (GROUP - 1) * half_rows), :]
     remote(part, part, w_send, w_forward, (dp, sibling)).wait_recv()
@@ -398,99 +409,91 @@
     for chunk in range(FEAT // WCHUNK):
         span = slice(chunk * WCHUNK, (chunk + 1) * WCHUNK)
         rounded = (gate[:, span] * tangent[:, span] * scale).astype(jnp.bfloat16)
-        for column in range(WCHUNK // LANES):
-            block = chunk * (WCHUNK // LANES) + column
-            spot = (block % 4) * COLUMNS + (block // 4) * LANES
-            direction[:, spot : spot + LANES] = rounded[:, column * LANES : (column + 1) * LANES]
-
-    def piece(group, part):
-        return pl.ds(pl.multiple_of(group * COLUMNS, COLUMNS) + part * LANES, LANES)
-
-    def cross(part, side):
-        return remote(
-            direction.at[:, piece(2 * (1 - z) + side, part)], crossed.at[:, piece(side, part)],
-            c_send, c_recv.at[part], (dp, z_pair),
-        )
-
-    def cross_wait(part):
-        both = crossed.at[:, pl.ds(0, 2 * LANES)]
-        return remote(both, both, c_send, c_recv.at[part], (dp, z_pair))
-
-    def spread(part, mine):
-        source = me if mine else z_pair
-
+        direction[:, span] = rounded
+
+    def turn(part):
+        return (part + z_hi) % 2
+
+    def send_direction(part):
         def one(step, carry):
-            partner = jnp.bitwise_xor(me, 4 * (step // 2) + step % 2)
-            if mine:
-                held = direction.at[:, piece(2 * z + partner % 2, part)]
-            else:
-                held = crossed.at[:, piece(partner % 2, part)]
+            partner = jnp.bitwise_xor(me, step)
             remote(
-                held, dir_in.at[rows_of(source, TOK), pl.ds(part * LANES, LANES)],
+                direction.at[:, lanes_of(4 * (partner // 4) + 2 * (partner % 2) + turn(part))],
+                dir_in.at[rows_of(me, TOK), pl.ds(part * LANES, LANES)],
                 d_send, d_recv.at[part], (dp, partner),
             ).start()
             return carry
 
-        lax.fori_loop(1, 8, one, 0)
-
-    def keep_part(part, mine):
-        source = me if mine else z_pair
-        held = direction.at[:, piece(me % 4, part)] if mine else crossed.at[:, piece(core, part)]
+        lax.fori_loop(1, GROUP, one, 0)
+        keep_part(part).start()
+
+    def keep_part(part):
         return pltpu.make_async_copy(
-            held, dir_in.at[rows_of(source, TOK), pl.ds(part * LANES, LANES)],
-            d_local.at[part, int(mine)],
+            direction.at[:, lanes_of(4 * x + 2 * core + turn(part))],
+            dir_in.at[rows_of(me, TOK), pl.ds(part * LANES, LANES)],
+            d_local.at[part],
         )
 
-    def pass_on(part):
-        cross_wait(part).wait_recv()
-        spread(part, False)
-        keep_part(part, False).start()
-
-    for part in range(4):
+    def finish_part(part):
+        span = slice(part * LANES, (part + 1) * LANES)
+        keep_part(part).wait()
+        others = dir_in.at[pl.ds(0, (GROUP - 1) * TOK), pl.ds(0, LANES)]
+        remote(others, others, d_send, d_recv.at[part], (dp, sibling)).wait_recv()
+        partial[span, :] = dot_columns(dir_in[:, span], heads_in[...]).astype(jnp.bfloat16)
+
+        def send_rows(step, carry):
+            other = jnp.bitwise_xor(y, step)
+            for side in range(2):
+                remote(
+                    partial.at[pl.ds(part * LANES, LANES), lanes_of(block_of(other, side))],
+                    stage_in.at[part, step - 1, side], h_send, h_recv.at[part],
+                    (jnp.bitwise_xor(dp, step), me),
+                ).start()
+            return carry
+
+        lax.fori_loop(1, 4, send_rows, 0)
+
+    def block_of(row, side):
+        return 2 * lax.rem(row + 8 - z - 2 * side, 4) + side
+
+    def reduce_part(part):
+        held = stage_in.at[part]
+        remote(held, held, h_send, h_recv.at[part], (dp, sibling)).wait_recv()
+        owner = 4 * x + 2 * core + turn(part)
         for side in range(2):
-            cross(part, side).start()
-    for part in range(4):
-        spread(part, True)
-        keep_part(part, True).start()
-        if part >= 1:
-            pass_on(part - 1)
-    pass_on(3)
-
-    cross_heads.wait_recv()
-    forward(1, jnp.bitwise_xor(place, 2)).start()
-    forward(0, place).wait_recv()
-    forward(1, place).wait_recv()
-
-    for part in range(4):
-        span = slice(part * LANES, (part + 1) * LANES)
-        keep_part(part, True).wait()
-        keep_part(part, False).wait()
-        every = dir_in.at[pl.ds(0, (GROUP - 2) * TOK), pl.ds(0, LANES)]
-        remote(every, every, d_send, d_recv.at[part], (dp, sibling)).wait_recv()
-        partial[span, :] = dot_columns(dir_in[:, span], heads_in[...]).astype(jnp.bfloat16)
-        owner = 4 * part + me % 4
-
-        def send_shares(step, carry, part=part, owner=owner):
-            block = jnp.bitwise_xor(step, z_hi)
-            row = heads_of(4 * x + block)
-            held = partial.at[pl.ds(part * LANES, LANES), lanes_of(block)]
+            block = block_of(y, side)
+            total = partial[part * LANES : (part + 1) * LANES, lanes_of(block)].astype(jnp.float32)
+            for step in range(3):
+                total = total + stage_in[part, step, side].astype(jnp.float32)
+            middle[part, side] = total.astype(jnp.bfloat16)
+            row = 4 * (block // 2) + y
             to_self = jnp.logical_and(row == dp, owner == me)
 
             @pl.when(jnp.logical_not(to_self))
             def _():
-                remote(held, shares.at[dp], g_send, g_recv, (row, owner)).start()
+                remote(
+                    middle.at[part, side], shares.at[z_hi], g_send, g_recv, (row, owner)
+                ).start()
 
             @pl.when(to_self)
             def _():
-                pltpu.make_async_copy(held, shares.at[dp], g_local).start()
-
-            return carry
-
-        lax.fori_loop(0, 4, send_shares, 0)
+                pltpu.make_async_copy(middle.at[part, side], shares.at[z_hi], g_local).start()
+
+    for part in range(PARTS):
+        send_direction(part)
+    for step in (1, 3, 2):
+        handed(step).wait_recv()
+        forward(step).start()
+    for step in range(4):
+        forward(step).wait_recv()
+    for part in range(PARTS):
+        finish_part(part)
+    for part in range(PARTS):
+        reduce_part(part)
 
     @pl.when(grad_self)
     def _():
-        part = shares.at[pl.ds(0, GROUP - 1)]
+        part = shares.at[pl.ds(0, SUMS - 1)]
         pltpu.make_async_copy(shares.at[0], shares.at[1], g_local).wait()
         whole = remote(part, part, g_send, g_recv, (dp, sibling))
         whole.wait_send()
@@ -505,21 +508,21 @@
     store_blended.wait()
     store_tan.wait()
     total = shares[0].astype(jnp.float32)
-    for sample in range(1, GROUP):
+    for sample in range(1, SUMS):
         total = total + shares[sample].astype(jnp.float32)
     grad_out[...] = -2.0 * total.T
 
-    every = dir_in.at[pl.ds(0, (GROUP - 2) * TOK), :]
-    remote(every, every, d_send, d_recv.at[0], (dp, sibling)).wait_send()
-    remote(crossed, crossed, c_send, c_recv.at[0], (dp, z_pair)).wait_send()
-    cross_heads.wait_send()
-    forward(0, place).wait_send()
-    forward(1, place).wait_send()
+    remote(stage_in, stage_in, h_send, h_recv.at[0], (dp, sibling)).wait_send()
+    others = dir_in.at[pl.ds(0, (GROUP - 1) * TOK), :]
+    remote(others, others, d_send, d_recv.at[0], (dp, sibling)).wait_send()
+    for step in (1, 3, 2):
+        handed(step).wait_send()
+    for step in range(4):
+        forward(step).wait_send()
     back.wait_send()
     part = w_in.at[pl.ds(0, 2 * (GROUP - 1) * half_rows), :]
     remote(part, part, w_send, w_forward, (dp, sibling)).wait_send()
-    for slot, (src, dst) in enumerate(keyed):
-        all_keys(slot, dst).wait_send()
+    all_keys(3, vt_in).wait_send()
     for slot, (src, dst) in enumerate(queried):
         part = dst.at[pl.ds(0, (GROUP - 1) * TOK), :]
         remote(part, part, send.at[4 + slot], recv_q.at[0], (dp, sibling)).wait_send()
@@ -558,15 +561,17 @@
             vmem((1, TOK, FEAT), half),
             vmem((TOK, FEAT), jnp.float32),
             vmem((TOK, FEAT), half),
-            vmem((TOKENS, QUARTER), half),
-            vmem((TOKENS, COLUMNS), half),
-            vmem((COLUMNS, QUARTER), half),
-            vmem((GROUP, LANES, LANES), half),
+            vmem((TOKENS, HALF_HEADS * LANES), half),
+            vmem((TOKENS, PARTS * LANES), half),
+            vmem((PARTS * LANES, HALF_HEADS * LANES), half),
+            vmem((SUMS, LANES, LANES), half),
             dma((6,)), dma((4,)), dma((GROUP // 2,)), dma((6,)), dma, dma, dma((2,)),
             dma, dma((GROUP,)), dma, dma, dma((2,)),
-            dma, dma, dma, dma((2,)), dma((2,)), dma, dma((4,)), dma((4, 2)),
-            dma, dma, dma, vmem((TOK, 2 * COLUMNS), half), dma, dma((4,)),
+            dma, dma((4,)), dma((4,)), dma((4,)), dma((4,)), dma, dma((PARTS,)), dma((PARTS,)),
+            dma, dma, dma,
             vmem((1, TOK, FEAT), half), vmem((1, TOK, FEAT), half), dma((2,)),
+            vmem((PARTS, 3, 2, LANES, LANES), half), vmem((PARTS, 2, LANES, LANES), half),
+            dma, dma((PARTS,)),
         ],
         compiler_params=pltpu.CompilerParams(
             collective_id=0, has_side_effects=True, vmem_limit_bytes=56 * 2**20

time: 123 us -> 118 us (0.959)
  the two profiles are of different devices: /device:TPU:6 before, /device:TPU:1 now
where the time goes in v3:
time: 118 us
  Pallas kernels  117 us (99%)
    pallas_call x1, Pallas kernels, whole(): pl.pallas_call(whole_kernel, out_shape=[jax.ShapeDtypeStruct((1, TOK, FEA...  115 us

profile of v3, /device:TPU:1, one launch (start us, length us, event | category | flops | bytes accessed | tf_op | source)
XLA Modules:
  0.0 117.5 jit_solution(17482314155247721594)
XLA Ops:
  0.6 114.7 %whole.1 = (bf16[1,128,2048]{2,1,0:T(8,128)(2,1)}, bf16[1,128,2048]{2,1,0:T(8,128)(2,1)}, f32[128,128]{1,0:T(8,128)}) custom-call(bf16[1,128,2048]{2,1,0:T(8,128)(2,1)} %q.1, bf16[1,144,2048]{2,1,0:T(8,128)(2,1)} %k.1, bf16[1,144,2048]{2,1,0:T(8,128)(2,1)} %v.1, bf16[1,128,2048]{2,1,0:T(8,128)(2,1)} %qt.1, bf16[1,144,2048]{2,1,0:T(8,128)(2,1)} %kt.1, ...), custom_call_target="tpu_custom_call" | custom-call | flops 10499999744 | bytes 20000000 | tf_op jit(solution)/shard_map/whole/pallas_call | solution.py:535
  115.3 2.2 %finish.1 = (bf16[1,128,2048]{2,1,0:T(8,128)(2,1)}, bf16[1,128,2048]{2,1,0:T(8,128)(2,1)}, f32[128,128]{1,0:T(8,128)}) custom-call(bf16[1,128,2048]{2,1,0:T(8,128)(2,1)} %get-tuple-element.6.refs_0_, bf16[1,128,2048]{2,1,0:T(8,128)(2,1)} %get-tuple-element.7.refs_1_, f32[128,128]{1,0:T(8,128)} %get-tuple-element.8.refs_2_), custom_call_target="tpu_custom_call" | custom-call | tf_op jit(solution)/shard_map/finish/pallas_call | solution.py:594

commit v4 on v3

--- a/solution.py
+++ b/solution.py
@@ -170,30 +170,6 @@
         part = dst.at[pl.ds(0, (GROUP - 1) * KEY_ROWS), :]
         return remote(part, part, send.at[slot], recv.at[slot], (dp, sibling))
 
-    for slot, (src, dst) in enumerate(keyed):
-        own(slot, src, dst, KEY_ROWS).start()
-        if slot >= 2:
-            all_keys(slot - 2, keyed[slot - 2][1]).wait_send()
-
-        def send_keys(step, carry, slot=slot, src=src, dst=dst):
-            partner = jnp.bitwise_xor(me, step)
-            remote(
-                src.at[0, :, lanes_of(heads_of(partner))], dst.at[rows_of(me, KEY_ROWS), :],
-                send.at[slot], recv.at[slot], (dp, partner),
-            ).start()
-            return carry
-
-        lax.fori_loop(1, GROUP, send_keys, 0)
-        if slot == 1:
-            send_weight_rows(dp)
-            wait_weight(second)
-            send_weight(second, (dp, z_pair))
-            send_weight_rows(second)
-    for slot, (src, dst) in enumerate(queried):
-        own(4 + slot, src, dst, TOK).start()
-
-    all_keys(2, v_in).wait_send()
-
     def send_queries(step, carry):
         partner = jnp.bitwise_xor(me, step)
         for slot, (src, dst) in enumerate(queried):
@@ -203,36 +179,36 @@
             ).start()
         return carry
 
-    lax.fori_loop(1, GROUP, send_queries, 0)
+    for slot, (src, dst) in enumerate(queried):
+        own(4 + slot, src, dst, TOK).start()
+    send_queries(1, 0)
+    for slot, (src, dst) in enumerate(keyed):
+        own(slot, src, dst, KEY_ROWS).start()
+        if slot >= 2:
+            all_keys(slot - 2, keyed[slot - 2][1]).wait_send()
+
+        def send_keys(step, carry, slot=slot, src=src, dst=dst):
+            partner = jnp.bitwise_xor(me, step)
+            remote(
+                src.at[0, :, lanes_of(heads_of(partner))], dst.at[rows_of(me, KEY_ROWS), :],
+                send.at[slot], recv.at[slot], (dp, partner),
+            ).start()
+            return carry
+
+        lax.fori_loop(1, GROUP, send_keys, 0)
+        if slot == 1:
+            send_weight_rows(dp)
+            wait_weight(second)
+            send_weight(second, (dp, z_pair))
+            send_weight_rows(second)
+
+    all_keys(2, v_in).wait_send()
+    lax.fori_loop(2, GROUP, send_queries, 0)
 
     lane = lax.broadcasted_iota(jnp.int32, (1, LANES), 1)
     low = lane < HEAD
     one = jnp.ones((), jnp.bfloat16)
     zero = jnp.zeros((), jnp.bfloat16)
-    for slot, (src, dst) in enumerate(keyed):
-        own(slot, src, dst, KEY_ROWS).wait()
-        all_keys(slot, dst).wait_recv()
-        if slot == 0:
-            keys[:, :LANES] = k_in[...]
-            forward_weight(second)
-            wait_weight(third)
-            send_weight(third, (next_dp, z_pair))
-            send_weight_rows(third)
-            forward_weight(third)
-        elif slot == 1:
-            keys[:, LANES:] = kt_in[...]
-        elif slot == 2:
-            values = v_in[...]
-            values_a[:, :LANES] = jnp.where(low, values, one)
-            values_b[:, :LANES] = jnp.where(low, one, values)
-            wait_weight(fourth)
-            send_weight_rows(fourth)
-            forward_weight(fourth)
-        else:
-            values = vt_in[...]
-            values_a[:, LANES:] = jnp.where(low, values, zero)
-            values_b[:, LANES:] = jnp.where(low, zero, values)
-
     tiles = KEYS // TILE
 
     def block_scores(rows, head):
@@ -251,6 +227,35 @@
                 piece = result[:BLOCK, column * LANES : (column + 1) * LANES]
                 peak = piece if peak is None else jnp.maximum(peak, piece)
         return peak
+
+    for slot, (src, dst) in enumerate(keyed):
+        own(slot, src, dst, KEY_ROWS).wait()
+        all_keys(slot, dst).wait_recv()
+        if slot == 0:
+            keys[:, :LANES] = k_in[...]
+            forward_weight(second)
+            wait_weight(third)
+            send_weight(third, (next_dp, z_pair))
+            send_weight_rows(third)
+            forward_weight(third)
+        elif slot == 1:
+            keys[:, LANES:] = kt_in[...]
+            for kind, (query_src, query_dst) in enumerate(queried):
+                own(4 + kind, query_src, query_dst, TOK).wait()
+            part = q_in.at[pl.ds(0, 2 * TOK), :]
+            remote(part, part, send.at[4], recv_q.at[chip], (dp, sibling)).wait_recv()
+            first_peaks = [block_scores(rows_of(chip, BLOCK), head) for head in range(2)]
+        elif slot == 2:
+            values = v_in[...]
+            values_a[:, :LANES] = jnp.where(low, values, one)
+            values_b[:, :LANES] = jnp.where(low, one, values)
+            wait_weight(fourth)
+            send_weight_rows(fourth)
+            forward_weight(fourth)
+        else:
+            values = vt_in[...]
+            values_a[:, LANES:] = jnp.where(low, values, zero)
+            values_b[:, LANES:] = jnp.where(low, zero, values)
 
     def block_values(head, peak):
         top = jnp.max(peak, axis=1, keepdims=True)
@@ -300,38 +305,10 @@
                     back_local.at[slot],
                 ).start()
 
-    def body(step, carry):
-        other = jnp.bitwise_xor(chip, step)
-
-        @pl.when(step == 0)
-        def _():
-            for slot, (src, dst) in enumerate(queried):
-                own(4 + slot, src, dst, TOK).wait()
-            part = q_in.at[pl.ds(0, 2 * TOK), :]
-            remote(part, part, send.at[4], recv_q.at[chip], (dp, sibling)).wait_recv()
-
-        @pl.when(step > 0)
-        def _():
-            part = q_in.at[pl.ds(0, 4 * TOK), :]
-            remote(part, part, send.at[4], recv_q.at[other], (dp, sibling)).wait_recv()
-
-        @pl.when(step == 2)
-        def _():
-            forward_weight_rows(dp)
-
-        @pl.when(step == 4)
-        def _():
-            forward_weight_rows(second)
-
-        @pl.when(step == 6)
-        def _():
-            forward_weight_rows(third)
-
+    def finish_block(other, step, both_peaks):
         rows = rows_of(other, BLOCK)
-        peak_a = block_scores(rows, 0)
-        peak_b = block_scores(rows, 1)
-        out_a, tan_a = block_values(0, peak_a)
-        out_b, tan_b = block_values(1, peak_b)
+        out_a, tan_a = block_values(0, both_peaks[0])
+        out_b, tan_b = block_values(1, both_peaks[1])
         heads_out[rows, :] = jnp.where(low, out_a, out_b).astype(jnp.bfloat16)
         heads_tan[rows, :] = jnp.where(low, tan_a, tan_b).astype(jnp.bfloat16)
         for side in range(2):
@@ -342,9 +319,33 @@
         def _():
             hand_over(rows)
 
+
+    def body(step, carry):
+        other = jnp.bitwise_xor(chip, step)
+
+        part = q_in.at[pl.ds(0, 4 * TOK), :]
+        remote(part, part, send.at[4], recv_q.at[other], (dp, sibling)).wait_recv()
+
+        @pl.when(step == 2)
+        def _():
+            forward_weight_rows(dp)
+
+        @pl.when(step == 4)
+        def _():
+            forward_weight_rows(second)
+
+        @pl.when(step == 6)
+        def _():
+            forward_weight_rows(third)
+
+        rows = rows_of(other, BLOCK)
+        peak_a = block_scores(rows, 0)
+        peak_b = block_scores(rows, 1)
+        finish_block(other, step, (peak_a, peak_b))
         return carry
 
-    lax.fori_loop(0, GROUP // 2, body, 0)
+    finish_block(chip, jnp.int32(0), first_peaks)
+    lax.fori_loop(1, GROUP // 2, body, 0)
 
     for slot, (held, first) in enumerate(((heads_out, 0), (heads_tan, TOK))):
         pltpu.make_async_copy(

time: 118 us -> 117 us (level)
  no operation moved by 1% of the time
where the time goes in v4:
time: 117 us
  Pallas kernels  116 us (99%)
    pallas_call x1, Pallas kernels, whole(): pl.pallas_call(whole_kernel, out_shape=[jax.ShapeDtypeStruct((1, TOK, FEA...  114 us

profile of v4, /device:TPU:1, one launch (start us, length us, event | category | flops | bytes accessed | tf_op | source)
XLA Modules:
  0.0 116.9 jit_solution(2864090398814519514)
XLA Ops:
  0.6 114.0 %whole.1 = (bf16[1,128,2048]{2,1,0:T(8,128)(2,1)}, bf16[1,128,2048]{2,1,0:T(8,128)(2,1)}, f32[128,128]{1,0:T(8,128)}) custom-call(bf16[1,128,2048]{2,1,0:T(8,128)(2,1)} %q.1, bf16[1,144,2048]{2,1,0:T(8,128)(2,1)} %k.1, bf16[1,144,2048]{2,1,0:T(8,128)(2,1)} %v.1, bf16[1,128,2048]{2,1,0:T(8,128)(2,1)} %qt.1, bf16[1,144,2048]{2,1,0:T(8,128)(2,1)} %kt.1, ...), custom_call_target="tpu_custom_call" | custom-call | flops 10499999744 | bytes 20000000 | tf_op jit(solution)/shard_map/whole/pallas_call | solution.py:536
  114.7 2.2 %finish.1 = (bf16[1,128,2048]{2,1,0:T(8,128)(2,1)}, bf16[1,128,2048]{2,1,0:T(8,128)(2,1)}, f32[128,128]{1,0:T(8,128)}) custom-call(bf16[1,128,2048]{2,1,0:T(8,128)(2,1)} %get-tuple-element.6.refs_0_, bf16[1,128,2048]{2,1,0:T(8,128)(2,1)} %get-tuple-element.7.refs_1_, f32[128,128]{1,0:T(8,128)} %get-tuple-element.8.refs_2_), custom_call_target="tpu_custom_call" | custom-call | tf_op jit(solution)/shard_map/finish/pallas_call | solution.py:595
